TPU v7x, 512 devices: a whole 4x8x8 slice. The times are simulated.
512 devices in a mesh: row: 32 (over x_hi, y, core), col: 16 (over x_lo, z).
Axes of the slice: x: 4 (x_hi: 2, x_lo: 2; x = x_hi * 2 + x_lo), y: 8, z: 8, core: 2. Of those that a mesh axis runs over, the one named last changes fastest.
Arguments:
- prior: bfloat16 [65536, 256], P(('row', 'col')), may hold values from 0.1 to 2
- inv_degree: float32 [65536], P(('row', 'col')), may hold values from 0.03125 to 0.125
- seed_rows: int32 [8192], P(('row', 'col')), may hold values from 0 to 127, as said below
- seed_scores: bfloat16 [8192, 256], P(('row', 'col')), may hold values from 0.1 to 2
- block_mask: int32 [36864, 128, 128], P(('row', 'col')), may hold values 0 or 1
- block_row: int32 [36864], P(('row', 'col')), may hold values from 0 to 31, as said below
- block_col: int32 [36864], P(('row', 'col')), may hold values from 0 to 15, as said below
- block_live: int32 [512], P(('row', 'col')), may hold values from 9 to 72, as said below
Outputs:
- labels: bfloat16 [65536, 256], P(('row', 'col'))
Inputs may be any that keep to these rules, and one draw needn't show every extreme that they name: `seed_rows`: within one device's 16 entries the indices are distinct. Within one device's 72 slots, the pairs (block_row, block_col) are distinct. `block_col`: see block_row. `block_live`: some device uses all 72 slots.
All inputs are finite; a program needn't handle non-finite values. No bound on the sum of `block_mask` on one device may be relied on, other than what follows from the above.
Results may differ from a plain program's by a relative error of at most 0.015.
Values may be sent and summed in bfloat16 or wider, within the bound.
A program may use at most 64 MiB of HBM per device.

v0:
```python
import jax
import jax.numpy as jnp
from jax import lax
from jax.sharding import PartitionSpec as P

ITERS = 2
MIX_RATE = 0.9


def local(prior, inv_degree, seed_rows, seed_scores, block_mask, block_row, block_col, block_live):
    docs_dev, width = prior.shape
    slots, side = (block_mask.shape[0], block_mask.shape[1])
    target_blocks = lax.axis_size("row") * docs_dev // side
    live = block_live[0]
    slot_ids = jnp.arange(slots, dtype=jnp.int32)
    weights = (block_mask * (slot_ids < live).astype(jnp.int32)[:, None, None]).astype(jnp.bfloat16)
    hits = (seed_rows[:, None] == jnp.arange(docs_dev, dtype=jnp.int32)[None, :]).astype(
        jnp.bfloat16
    )
    seeded = jnp.dot(hits.T, seed_scores, preferred_element_type=jnp.float32)
    covered = jnp.sum(hits.astype(jnp.float32), axis=0) > 0.5
    base = (1.0 - MIX_RATE) * prior.astype(jnp.float32)
    factor = MIX_RATE * inv_degree[:, None]
    labels = prior
    for step in range(ITERS):
        sources = lax.all_gather(labels, "col", axis=0, tiled=True)
        src_blocks = sources.reshape(-1, side, width)
        picked = jnp.take(src_blocks, block_col, axis=0)
        products = jnp.einsum("sij,sjl->sil", weights, picked, preferred_element_type=jnp.float32)
        summed = jnp.zeros((target_blocks, side, width), jnp.float32).at[block_row].add(products)
        summed = summed.reshape(target_blocks * side, width)
        sums = lax.psum_scatter(
            summed.astype(jnp.bfloat16), "row", scatter_dimension=0, tiled=True
        ).astype(jnp.float32)
        fresh = factor * sums + base
        labels = jnp.where(covered[:, None], seeded, fresh).astype(jnp.bfloat16)
    return labels


def solution(mesh):
    return jax.shard_map(
        local,
        mesh=mesh,
        in_specs=(
            P(("row", "col"), None),
            P(("row", "col")),
            P(("row", "col")),
            P(("row", "col"), None),
            P(("row", "col"), None, None),
            P(("row", "col")),
            P(("row", "col")),
            P(("row", "col")),
        ),
        out_specs=P(("row", "col"), None),
        check_vma=False,
    )
```

profile of v0, /device:TPU:16, one launch (start us, length us, event | category | flops | bytes accessed | tf_op | source)
XLA Modules:
  0.0 508.4 jit_solution(6479234486084292138)
XLA Ops:
  6.5 0.0 copy-start
  6.5 0.0 all-gather.3.cloned.1.call-start
  6.5 0.7 all-gather.3.cloned.1.call-update
  7.3 0.0 reduce-scatter.3.cloned.1.call-start
  8.0 0.7 compare_select_fusion
  8.6 0.7 compare_select_fusion.1
  9.3 0.7 compare_and_fusion
  9.9 76.6 %all-gather.3.cloned.1.call-done = bf16[2048,256]{1,0:T(8,128)(2,1)} async-done(((bf16[128,256]{1,0:T(8,128)(2,1)}), bf16[2048,256]{1,0:T(8,128)(2,1)}) %all-gather.3.cloned.1.call-update) | async-done | bytes 1048592 | tf_op jit(solution)/shard_map/all_gather | solution.py:26
  86.5 6.8 %gather_fusion = bf16[72,128,256]{2,1,0:T(8,128)(2,1)} fusion(bf16[16,128,256]{2,1,0:T(8,128)(2,1)} %bitcast.7, s32[1024]{0:T(1024)S(1)} %pad_clamp_fusion), kind=kCustom, calls=%fused_computation.clone | custom fusion | bytes 9437472 | tf_op jit(solution)/shard_map/jit(_take)/gather | solution.py:28
  93.3 8.9 %fusion.2 = f32[72,128,256]{2,1,0:T(8,128)} fusion(bf16[72,128,256]{2,1,0:T(8,128)(2,1)} %gather_fusion, pred[72]{0:T(512)(128)(4,1)S(1)} %get-tuple-element.8, s32[72,128,128]{2,1,0:T(8,128)} %param.14, s32[72]{0:T(128)S(1)} %get-tuple-element.9), kind=kOutput, calls=%fused_computation.6 | convolution fusion | flops 608698368 | bytes 18874728 | tf_op jit(solution)/shard_map/sij,sjl->sil/dot_general | solution.py:29
  102.2 2.6 broadcast.23.clone
  104.8 23.3 %scatter_fusion = f32[32,128,256]{2,1,0:T(8,128)} fusion(f32[32,128,256]{2,1,0:T(8,128)} %broadcast.23.clone, s32[72]{0:T(128)S(1)} %compare_select_fusion.1, f32[72,128,256]{2,1,0:T(8,128)} %fusion.2), kind=kCustom, calls=%fused_computation.2 | custom fusion | flops 2359296 | bytes 28311840 | tf_op jit(solution)/shard_map/scatter-add | solution.py:30
  128.1 0.0 copy-start.3
  128.1 0.0 copy-start.2
  128.1 0.0 copy-start.1
  128.1 3.8 convert_element_type.47
  131.9 0.0 reduce-scatter.3.cloned.1.call-update
  131.9 0.0 all-gather.5.cloned.1.call-start
  132.0 0.0 copy-done.3
  132.0 0.1 convert_reduce_fusion
  132.1 0.0 copy-done.2
  132.1 124.6 %reduce-scatter.3.cloned.1.call-done = bf16[128,256]{1,0:T(8,128)(2,1)} async-done(((bf16[4096,256]{1,0:T(8,128)(2,1)}), bf16[128,256]{1,0:T(8,128)(2,1)}) %reduce-scatter.3.cloned.1.call-update) | async-done | bytes 65552 | tf_op jit(solution)/shard_map/reduce_scatter | solution.py:32
  256.7 0.0 copy-done
  256.7 0.0 copy-done.1
  256.7 1.8 select_convert_fusion.1
  258.5 0.0 all-gather.5.cloned.1.call-update
  258.5 0.0 reduce-scatter.5.cloned.1.call-start
  258.5 71.6 %all-gather.5.cloned.1.call-done = bf16[2048,256]{1,0:T(8,128)(2,1)} async-done(((bf16[128,256]{1,0:T(8,128)(2,1)}), bf16[2048,256]{1,0:T(8,128)(2,1)}) %all-gather.5.cloned.1.call-update) | async-done | bytes 1048592 | tf_op jit(solution)/shard_map/all_gather | solution.py:26
  330.1 6.8 %gather_fusion.1 = bf16[72,128,256]{2,1,0:T(8,128)(2,1)} fusion(bf16[16,128,256]{2,1,0:T(8,128)(2,1)} %bitcast.8, s32[1024]{0:T(1024)S(1)} %pad_clamp_fusion), kind=kCustom, calls=%fused_computation.1.clone | custom fusion | bytes 9437472 | tf_op jit(solution)/shard_map/jit(_take)/gather | solution.py:28
  337.0 8.9 %fusion = f32[72,128,256]{2,1,0:T(8,128)} fusion(bf16[72,128,256]{2,1,0:T(8,128)(2,1)} %gather_fusion.1, pred[72]{0:T(512)(128)(4,1)S(1)} %get-tuple-element.8, s32[72,128,128]{2,1,0:T(8,128)} %param.14, s32[72]{0:T(128)S(1)} %get-tuple-element.9), kind=kOutput, calls=%fused_computation.4 | convolution fusion | flops 608698368 | bytes 18874728 | tf_op jit(solution)/shard_map/sij,sjl->sil/dot_general | solution.py:29
  345.8 2.6 broadcast.23
  348.4 23.3 %scatter_fusion.1 = f32[32,128,256]{2,1,0:T(8,128)} fusion(f32[32,128,256]{2,1,0:T(8,128)} %broadcast.23, s32[72]{0:T(128)S(1)} %compare_select_fusion.1, f32[72,128,256]{2,1,0:T(8,128)} %fusion), kind=kCustom, calls=%fused_computation.3 | custom fusion | flops 2359296 | bytes 28311840 | tf_op jit(solution)/shard_map/scatter-add | solution.py:30
  371.7 3.8 convert_element_type.52
  375.5 0.0 reduce-scatter.5.cloned.1.call-update
  375.5 124.8 %reduce-scatter.5.cloned.1.call-done = bf16[128,256]{1,0:T(8,128)(2,1)} async-done(((bf16[4096,256]{1,0:T(8,128)(2,1)}), bf16[128,256]{1,0:T(8,128)(2,1)}) %reduce-scatter.5.cloned.1.call-update) | async-done | bytes 65552 | tf_op jit(solution)/shard_map/reduce_scatter | solution.py:32
  500.3 1.6 select_convert_fusion
  (3 shorter events, 0.0 us)
Async XLA Ops:
  6.5 250.2 %copy-start = (bf16[16,256]{1,0:T(8,128)(2,1)S(1)}, bf16[16,256]{1,0:T(8,128)(2,1)}, u32[]{:S(2)}) copy-start(bf16[16,256]{1,0:T(8,128)(2,1)} %param.13) | copy-start | bytes 24580
  6.5 80.0 %all-gather.3.cloned.1.call-start = ((), (), s32[]{:S(2)}) async-start(), calls=%async_computation.2 | async-start | bytes 1114112 | tf_op jit(solution)/shard_map/all_gather | solution.py:26
  7.3 249.4 %reduce-scatter.3.cloned.1.call-start = ((), (), s32[]{:S(2)}) async-start(), calls=%async_computation.3 | async-start | bytes 2162688 | tf_op jit(solution)/shard_map/reduce_scatter | solution.py:32
  128.1 3.9 copy-start.3
  128.1 4.0 copy-start.2
  128.1 128.6 %copy-start.1 = (bf16[128,256]{1,0:T(8,128)(2,1)S(1)}, bf16[128,256]{1,0:T(8,128)(2,1)}, u32[]{:S(2)}) copy-start(bf16[128,256]{1,0:T(8,128)(2,1)} %param.10) | copy-start | bytes 196612
  131.9 198.2 %all-gather.5.cloned.1.call-start = ((), (), s32[]{:S(2)}) async-start(), calls=%async_computation.4 | async-start | bytes 1114112 | tf_op jit(solution)/shard_map/all_gather | solution.py:26
  258.5 241.8 %reduce-scatter.5.cloned.1.call-start = ((), (), s32[]{:S(2)}) async-start(), calls=%async_computation.5 | async-start | bytes 2162688 | tf_op jit(solution)/shard_map/reduce_scatter | solution.py:32
Sparse Core Ops, SparseCore 0:
  9.4 77.0 all-gather.2
  132.1 124.5 reduce-scatter.2
  259.0 71.0 all-gather.4
  375.6 124.6 reduce-scatter.4
where the time goes:
time: 509 us; the launch traced here: 508 us
  waiting for transfers between devices  398 us (78%)
  other arithmetic  57.9 us (11%)
  matrix products  19.5 us (4%)
  local copies, waits for them, and re-layouts  18.8 us (4%)
  between operations  13.8 us (3%)
    reduce_scatter x2, waiting for transfers between devices, local(): lax.psum_scatter(summed.astype(jnp.bfloat16), 'row', scatter_dimension=0,...  249 us
    all_gather x2, waiting for transfers between devices, local(): sources = lax.all_gather(labels, 'col', axis=0, tiled=True)  148 us
    scatter-add x2, other arithmetic, local(): jnp.zeros((target_blocks, side, width), jnp.float32).at[block_row]  46.6 us
    dot_general x2, matrix products, local(): jnp.einsum('sij,sjl->sil', weights, picked, preferred_element_type=jnp.fl...  17.7 us
    gather x2, local copies, waits for them, and re-layouts, local(): picked = jnp.take(src_blocks, block_col, axis=0)  13.6 us
  transfers between devices with their start and end apart: 4, of which 4 were waited for; matrix products, arithmetic and copies ran while one was open for 0% of the time, Pallas kernels for 0%

commit v1 on v0

--- a/solution.py
+++ b/solution.py
@@ -23,7 +23,9 @@
     factor = MIX_RATE * inv_degree[:, None]
     labels = prior
     for step in range(ITERS):
-        sources = lax.all_gather(labels, "col", axis=0, tiled=True)
+        sources = jnp.concatenate(
+            lax.all_to_all(jnp.stack([labels] * lax.axis_size("col")), "col", 0, 0), axis=0
+        )
         src_blocks = sources.reshape(-1, side, width)
         picked = jnp.take(src_blocks, block_col, axis=0)
         products = jnp.einsum("sij,sjl->sil", weights, picked, preferred_element_type=jnp.float32)

time: 509 us -> 423 us (0.83)
  waiting for transfers between devices: 398 us -> 273 us
  blocking collectives: 0 us -> 29.1 us
  starting transfers between devices: 0.12 us -> 11.4 us
    all_gather x2 -> x0, waiting for transfers between devices: 148 us -> none  [local(): sources = lax.all_gather(labels, 'col', axis=0, tiled=True)]
    all_to_all x0 -> x1, blocking collectives: none -> 29.1 us  [local(): lax.all_to_all(jnp.stack([labels] * lax.axis_size('col')), 'col', 0, 0)]
    all_to_all x0 -> x1, waiting for transfers between devices: none -> 24.4 us  [local(): lax.all_to_all(jnp.stack([labels] * lax.axis_size('col')), 'col', 0, 0)]
    all_to_all x0 -> x1, starting transfers between devices: none -> 11.3 us  [local(): lax.all_to_all(jnp.stack([labels] * lax.axis_size('col')), 'col', 0, 0)]
  transfers between devices with their start and end apart: 4 -> 3, of which waited for: 4 -> 3; matrix products, arithmetic and copies ran while one was open for 0% -> 0% of each run, Pallas kernels for 0% -> 0%
where the time goes in v1:
time: 423 us; the launch traced here: 422 us
  waiting for transfers between devices  273 us (65%)
  other arithmetic  58.1 us (14%)
  blocking collectives  29.1 us (7%)
  matrix products  18.8 us (4%)
  local copies, waits for them, and re-layouts  18.3 us (4%)
  between operations  14.1 us (3%)
  starting transfers between devices  11.4 us (3%)
    reduce_scatter x2, waiting for transfers between devices, local(): lax.psum_scatter(summed.astype(jnp.bfloat16), 'row', scatter_dimension=0,...  248 us
    scatter-add x2, other arithmetic, local(): jnp.zeros((target_blocks, side, width), jnp.float32).at[block_row]  46.7 us
    all_to_all x1, blocking collectives, local(): lax.all_to_all(jnp.stack([labels] * lax.axis_size('col')), 'col', 0, 0)  29.1 us
    all_to_all x1, waiting for transfers between devices, local(): lax.all_to_all(jnp.stack([labels] * lax.axis_size('col')), 'col', 0, 0)  24.4 us
    dot_general x2, matrix products, local(): jnp.einsum('sij,sjl->sil', weights, picked, preferred_element_type=jnp.fl...  17.7 us
    all_to_all x1, starting transfers between devices, local(): lax.all_to_all(jnp.stack([labels] * lax.axis_size('col')), 'col', 0, 0)  11.3 us
    gather x2, local copies, waits for them, and re-layouts, local(): picked = jnp.take(src_blocks, block_col, axis=0)  11.2 us
  transfers between devices with their start and end apart: 3, of which 3 were waited for; matrix products, arithmetic and copies ran while one was open for 0% of the time, Pallas kernels for 0%

profile of v1, /device:TPU:16, one launch (start us, length us, event | category | flops | bytes accessed | tf_op | source)
XLA Modules:
  0.0 422.5 jit_solution(10866430082161223295)
XLA Ops:
  6.5 0.0 copy-start
  6.5 1.9 stack.4
  8.5 11.3 %all-to-all-start = ((bf16[16,128,256]{2,1,0:T(8,128)(2,1)}), bf16[16,128,256]{2,1,0:T(8,128)(2,1)S(1)}, u32[]{:S(2)}, u32[]{:S(2)}) async-start(bf16[16,128,256]{2,1,0:T(8,128)(2,1)} %stack.4), calls=%async_computation | async-start | bytes 2097152 | tf_op jit(solution)/shard_map/all_to_all | solution.py:27
  19.8 0.0 reduce-scatter.3.cloned.1.call-start
  20.5 0.7 compare_select_fusion
  21.2 0.7 compare_select_fusion.1
  21.9 0.7 compare_and_fusion
  22.5 24.4 %all-to-all-done = bf16[16,128,256]{2,1,0:T(8,128)(2,1)S(1)} async-done(((bf16[16,128,256]{2,1,0:T(8,128)(2,1)}), bf16[16,128,256]{2,1,0:T(8,128)(2,1)S(1)}, u32[]{:S(2)}, u32[]{:S(2)}) %all-to-all-start) | async-done | bytes 1048608 | tf_op jit(solution)/shard_map/all_to_all | solution.py:27
  46.9 5.6 %gather_fusion = bf16[72,128,256]{2,1,0:T(8,128)(2,1)} fusion(bf16[16,128,256]{2,1,0:T(8,128)(2,1)S(1)} %all-to-all-done, s32[1024]{0:T(1024)S(1)} %pad_clamp_fusion), kind=kCustom, calls=%fused_computation.clone | custom fusion | bytes 9437472 | tf_op jit(solution)/shard_map/jit(_take)/gather | solution.py:30
  52.5 8.9 %fusion.2 = f32[72,128,256]{2,1,0:T(8,128)} fusion(bf16[72,128,256]{2,1,0:T(8,128)(2,1)} %gather_fusion, pred[72]{0:T(512)(128)(4,1)S(1)} %get-tuple-element.8, s32[72,128,128]{2,1,0:T(8,128)} %param.14, s32[72]{0:T(128)S(1)} %get-tuple-element.9), kind=kOutput, calls=%fused_computation.6 | convolution fusion | flops 608698368 | bytes 18874728 | tf_op jit(solution)/shard_map/sij,sjl->sil/dot_general | solution.py:31
  61.4 2.6 broadcast.27.clone
  63.9 23.4 %scatter_fusion = f32[32,128,256]{2,1,0:T(8,128)} fusion(f32[32,128,256]{2,1,0:T(8,128)} %broadcast.27.clone, s32[72]{0:T(128)S(1)} %compare_select_fusion.1, f32[72,128,256]{2,1,0:T(8,128)} %fusion.2), kind=kCustom, calls=%fused_computation.2 | custom fusion | flops 2359296 | bytes 28311840 | tf_op jit(solution)/shard_map/scatter-add | solution.py:32
  87.3 0.0 copy-start.3
  87.3 0.0 copy-start.2
  87.3 0.0 copy-start.1
  87.3 3.9 convert_element_type.47
  91.1 0.0 reduce-scatter.3.cloned.1.call-update
  91.2 0.0 reduce-scatter.5.cloned.1.call-start
  91.2 0.0 copy-done.3
  91.2 0.1 convert_reduce_fusion
  91.3 0.0 copy-done.2
  91.3 124.8 %reduce-scatter.3.cloned.1.call-done = bf16[128,256]{1,0:T(8,128)(2,1)} async-done(((bf16[4096,256]{1,0:T(8,128)(2,1)}), bf16[128,256]{1,0:T(8,128)(2,1)}) %reduce-scatter.3.cloned.1.call-update) | async-done | bytes 65552 | tf_op jit(solution)/shard_map/reduce_scatter | solution.py:34
  216.2 0.0 copy-done
  216.2 0.0 copy-done.1
  216.2 1.1 select_convert_fusion.1
  217.3 0.1 stack.5
  217.4 29.1 %all_to_all.10 = bf16[16,128,256]{2,1,0:T(8,128)(2,1)S(1)} all-to-all(bf16[16,128,256]{2,1,0:T(8,128)(2,1)S(1)} %stack.5), channel_id=1, replica_groups=mesh['row'=32,'col'=16] {'col'}, dimensions={0} | all-to-all | bytes 2097152 | tf_op jit(solution)/shard_map/all_to_all | solution.py:27
  246.5 5.6 %gather_fusion.1 = bf16[72,128,256]{2,1,0:T(8,128)(2,1)} fusion(bf16[16,128,256]{2,1,0:T(8,128)(2,1)S(1)} %all_to_all.10, s32[1024]{0:T(1024)S(1)} %pad_clamp_fusion), kind=kCustom, calls=%fused_computation.1.clone | custom fusion | bytes 9437472 | tf_op jit(solution)/shard_map/jit(_take)/gather | solution.py:30
  252.1 8.9 %fusion = f32[72,128,256]{2,1,0:T(8,128)} fusion(bf16[72,128,256]{2,1,0:T(8,128)(2,1)} %gather_fusion.1, pred[72]{0:T(512)(128)(4,1)S(1)} %get-tuple-element.8, s32[72,128,128]{2,1,0:T(8,128)} %param.14, s32[72]{0:T(128)S(1)} %get-tuple-element.9), kind=kOutput, calls=%fused_computation.4 | convolution fusion | flops 608698368 | bytes 18874728 | tf_op jit(solution)/shard_map/sij,sjl->sil/dot_general | solution.py:31
  260.9 2.6 broadcast.27
  263.5 23.4 %scatter_fusion.1 = f32[32,128,256]{2,1,0:T(8,128)} fusion(f32[32,128,256]{2,1,0:T(8,128)} %broadcast.27, s32[72]{0:T(128)S(1)} %compare_select_fusion.1, f32[72,128,256]{2,1,0:T(8,128)} %fusion), kind=kCustom, calls=%fused_computation.3 | custom fusion | flops 2359296 | bytes 28311840 | tf_op jit(solution)/shard_map/scatter-add | solution.py:32
  286.8 3.8 convert_element_type.52
  290.7 0.0 reduce-scatter.5.cloned.1.call-update
  290.7 123.4 %reduce-scatter.5.cloned.1.call-done = bf16[128,256]{1,0:T(8,128)(2,1)} async-done(((bf16[4096,256]{1,0:T(8,128)(2,1)}), bf16[128,256]{1,0:T(8,128)(2,1)}) %reduce-scatter.5.cloned.1.call-update) | async-done | bytes 65552 | tf_op jit(solution)/shard_map/reduce_scatter | solution.py:34
  414.1 1.6 select_convert_fusion
  (3 shorter events, 0.0 us)
Async XLA Ops:
  6.5 209.6 %copy-start = (bf16[16,256]{1,0:T(8,128)(2,1)S(1)}, bf16[16,256]{1,0:T(8,128)(2,1)}, u32[]{:S(2)}) copy-start(bf16[16,256]{1,0:T(8,128)(2,1)} %param.13) | copy-start | bytes 24580
  8.5 38.4 %all-to-all-start = ((bf16[16,128,256]{2,1,0:T(8,128)(2,1)}), bf16[16,128,256]{2,1,0:T(8,128)(2,1)S(1)}, u32[]{:S(2)}, u32[]{:S(2)}) async-start(bf16[16,128,256]{2,1,0:T(8,128)(2,1)} %stack.4), calls=%async_computation | async-start | bytes 2097152 | tf_op jit(solution)/shard_map/all_to_all | solution.py:27
  19.8 196.3 %reduce-scatter.3.cloned.1.call-start = ((), (), s32[]{:S(2)}) async-start(), calls=%async_computation.4 | async-start | bytes 2162688 | tf_op jit(solution)/shard_map/reduce_scatter | solution.py:34
  87.3 3.9 copy-start.3
  87.3 4.1 copy-start.2
  87.3 128.9 %copy-start.1 = (bf16[128,256]{1,0:T(8,128)(2,1)S(1)}, bf16[128,256]{1,0:T(8,128)(2,1)}, u32[]{:S(2)}) copy-start(bf16[128,256]{1,0:T(8,128)(2,1)} %param.10) | copy-start | bytes 196612
  91.2 322.9 %reduce-scatter.5.cloned.1.call-start = ((), (), s32[]{:S(2)}) async-start(), calls=%async_computation.5 | async-start | bytes 2162688 | tf_op jit(solution)/shard_map/reduce_scatter | solution.py:34
Sparse Core Ops, SparseCore 0:
  91.3 124.8 reduce-scatter.2
  290.8 123.2 reduce-scatter.4
